TPU v7x, 32 devices: a whole 2x2x4 slice. The times are simulated.
32 devices in a mesh: dp: 8 (over z, x), tensor: 4 (over y, core).
Axes of the slice: x: 2, y: 2, z: 4, core: 2. Of those that a mesh axis runs over, the one named last changes fastest.
Arguments:
- images: bfloat16 [24, 729, 1152], P('dp', None, 'tensor'), may hold values from -6 to 6
- image_count: int32 [8], P('dp'), may hold values from 2 to 3, as said below
- attn_gain: float32 [1152], replicated, may hold values from 0.5 to 1.5
- attn_shift: float32 [1152], replicated, may hold values from -1.8 to 1.8
- query_weight: bfloat16 [1152, 1152], P('dp', 'tensor'), may hold values from -0.25 to 0.25
- query_bias: float32 [1152], P('tensor'), may hold values from -3 to 3
- key_weight: bfloat16 [1152, 1152], P('dp', 'tensor'), may hold values from -0.25 to 0.25
- value_weight: bfloat16 [1152, 1152], P('dp', 'tensor'), may hold values from -0.1875 to 0.1875
- value_bias: float32 [1152], P('tensor'), may hold values from -3 to 3
- output_weight: bfloat16 [1152, 1152], P('tensor', 'dp'), may hold values from -1 to 1
- output_bias: float32 [1152], P('tensor'), may hold values from -3 to 3
- mlp_gain: float32 [1152], replicated, may hold values from 0.5 to 1.5
- mlp_shift: float32 [1152], replicated, may hold values from -1.8 to 1.8
- up_weight: bfloat16 [1152, 4304], P('dp', 'tensor'), may hold values from -0.1875 to 0.1875
- up_bias: float32 [4304], P('tensor'), may hold values from -3 to 3
- down_weight: bfloat16 [4304, 1152], P('tensor', 'dp'), may hold values from -0.125 to 0.125
- down_bias: float32 [1152], P('tensor'), may hold values from -3 to 3
- cotangent: bfloat16 [24, 729, 1152], P('dp', None, 'tensor'), may hold values from -6 to 6
Outputs:
- layer_out: bfloat16 [24, 729, 1152], P('dp', None, 'tensor')
- image_grad: bfloat16 [24, 729, 1152], P('dp', None, 'tensor')
- attn_gain_grad: float32 [1152], P('tensor')
- attn_shift_grad: float32 [1152], P('tensor')
- query_weight_grad: float32 [1152, 1152], P('dp', 'tensor')
- query_bias_grad: float32 [1152], P('tensor')
- key_weight_grad: float32 [1152, 1152], P('dp', 'tensor')
- value_weight_grad: float32 [1152, 1152], P('dp', 'tensor')
- value_bias_grad: float32 [1152], P('tensor')
- output_weight_grad: float32 [1152, 1152], P('tensor', 'dp')
- output_bias_grad: float32 [1152], P('tensor')
- mlp_gain_grad: float32 [1152], P('tensor')
- mlp_shift_grad: float32 [1152], P('tensor')
- up_weight_grad: float32 [1152, 4304], P('dp', 'tensor')
- up_bias_grad: float32 [4304], P('tensor')
- down_weight_grad: float32 [4304, 1152], P('tensor', 'dp')
- down_bias_grad: float32 [1152], P('tensor')
Inputs may be any that keep to these rules, and one draw needn't show every extreme that they name: Slots 0 to image_count - 1 of a data position hold its images; some position has 3 images and some has 2.
All inputs are finite; a program needn't handle non-finite values.
Results may differ from a plain program's by a relative error of at most 0.017.
Values may be sent and summed in bfloat16 or wider, within the bound.
No kernel may reach another device: no remote copies, remote signals or barrier semaphores. Data moves between devices by JAX's collectives and lax.ppermute only.
A program may use at most 256 MiB of HBM per device.

v0:
```python
import math
import jax
import jax.numpy as jnp
from jax import lax
from jax.sharding import PartitionSpec as P

HDIM = 72
EPSILON = 1e-06


def gelu_tanh(value):
    return jax.nn.gelu(value, approximate=True)


def fetch_weights(query_weight, key_weight, value_weight, up_weight, output_weight, down_weight):
    row_parts = (
        lax.all_gather(query_weight, "dp", axis=0, tiled=True),
        lax.all_gather(key_weight, "dp", axis=0, tiled=True),
        lax.all_gather(value_weight, "dp", axis=0, tiled=True),
        lax.all_gather(up_weight, "dp", axis=0, tiled=True),
    )
    col_parts = (
        lax.all_gather(output_weight, "dp", axis=1, tiled=True),
        lax.all_gather(down_weight, "dp", axis=1, tiled=True),
    )
    return tuple(row_parts) + tuple(col_parts)


def normalize(rows):
    centred = rows - jnp.mean(rows, axis=1, keepdims=True)
    inverse = lax.rsqrt(jnp.mean(centred * centred, axis=1, keepdims=True) + EPSILON)
    return (centred * inverse, inverse)


def norm_back(grad_share, normed_share, inverse, gain_share):
    scaled = grad_share * gain_share
    totals = lax.psum((jnp.sum(scaled, axis=1), jnp.sum(scaled * normed_share, axis=1)), "tensor")
    width = grad_share.shape[1] * lax.axis_size("tensor")
    first_mean = totals[0][:, None] / width
    second_mean = totals[1][:, None] / width
    return inverse * (scaled - first_mean - normed_share * second_mean)


def split_heads(rows):
    return rows.reshape(rows.shape[0], -1, HDIM).transpose(1, 0, 2)


def merge_heads(blocks):
    return blocks.transpose(1, 0, 2).reshape(blocks.shape[1], -1)


def column_share(whole, start, width):
    return lax.dynamic_slice_in_dim(whole, start, width, whole.ndim - 1)


def local(
    images,
    image_count,
    attn_gain,
    attn_shift,
    query_weight,
    query_bias,
    key_weight,
    value_weight,
    value_bias,
    output_weight,
    output_bias,
    mlp_gain,
    mlp_shift,
    up_weight,
    up_bias,
    down_weight,
    down_bias,
    cotangent,
):
    share_width = images.shape[2]
    share_start = lax.axis_index("tensor") * share_width
    attn_gain_share = column_share(attn_gain, share_start, share_width)
    mlp_gain_share = column_share(mlp_gain, share_start, share_width)
    score_scale = 1.0 / math.sqrt(HDIM)
    grads_sum = None
    out_slots = []
    grad_slots = []
    for slot_index in range(images.shape[0]):
        weights_now = fetch_weights(
            query_weight, key_weight, value_weight, up_weight, output_weight, down_weight
        )
        query_full, key_full, value_full, up_full, output_full, down_full = weights_now
        live_flag = (image_count[0] > slot_index).astype(jnp.float32)
        rows_pair = (
            lax.all_gather(images[slot_index], "tensor", axis=1, tiled=True),
            lax.all_gather(cotangent[slot_index], "tensor", axis=1, tiled=True),
        )
        input_full = rows_pair[0].astype(jnp.float32)
        grad_full = rows_pair[1].astype(jnp.float32) * live_flag
        grad_low = grad_full.astype(jnp.bfloat16)
        input_share = images[slot_index].astype(jnp.float32)
        grad_share = cotangent[slot_index].astype(jnp.float32) * live_flag
        normed1, inverse1 = normalize(input_full)
        attn_in = (normed1 * attn_gain + attn_shift).astype(jnp.bfloat16)
        query_low = (
            jnp.dot(attn_in, query_full, preferred_element_type=jnp.float32) + query_bias
        ).astype(jnp.bfloat16)
        key_low = jnp.dot(attn_in, key_full, preferred_element_type=jnp.float32).astype(
            jnp.bfloat16
        )
        value_low = (
            jnp.dot(attn_in, value_full, preferred_element_type=jnp.float32) + value_bias
        ).astype(jnp.bfloat16)
        query_heads = split_heads(query_low)
        key_heads = split_heads(key_low)
        value_heads = split_heads(value_low)
        scores = (
            jnp.einsum("hqd,hkd->hqk", query_heads, key_heads, preferred_element_type=jnp.float32)
            * score_scale
        )
        row_max = jnp.max(scores, axis=-1, keepdims=True)
        expo = jnp.exp(scores - row_max)
        prob_total = jnp.sum(expo, axis=-1, keepdims=True)
        log_total = row_max + jnp.log(prob_total)
        probs_low = (expo / prob_total).astype(jnp.bfloat16)
        mixed_heads = jnp.einsum(
            "hqk,hkd->hqd", probs_low, value_heads, preferred_element_type=jnp.float32
        )
        mixed_low = merge_heads(mixed_heads).astype(jnp.bfloat16)
        attn_partial = jnp.dot(mixed_low, output_full, preferred_element_type=jnp.float32)
        attn_share = lax.psum_scatter(attn_partial, "tensor", scatter_dimension=1, tiled=True)
        hidden1_share = input_share + attn_share + output_bias
        hidden1_full = lax.all_gather(hidden1_share, "tensor", axis=1, tiled=True)
        normed2, inverse2 = normalize(hidden1_full)
        mlp_in = (normed2 * mlp_gain + mlp_shift).astype(jnp.bfloat16)
        pre_act = jnp.dot(mlp_in, up_full, preferred_element_type=jnp.float32) + up_bias
        activ, gelu_pull = jax.vjp(gelu_tanh, pre_act)
        activ_low = activ.astype(jnp.bfloat16)
        mlp_partial = jnp.dot(activ_low, down_full, preferred_element_type=jnp.float32)
        mlp_share = lax.psum_scatter(
            mlp_partial.astype(jnp.bfloat16), "tensor", scatter_dimension=1, tiled=True
        ).astype(jnp.float32)
        out_slots.append(((hidden1_share + mlp_share + down_bias) * live_flag).astype(jnp.bfloat16))
        down_grad = jnp.einsum("sf,sd->fd", activ_low, grad_low, preferred_element_type=jnp.float32)
        hidden_grad = jnp.einsum(
            "sd,fd->sf", grad_low, down_full, preferred_element_type=jnp.float32
        )
        pre_grad = gelu_pull(hidden_grad)[0].astype(jnp.bfloat16)
        up_grad = jnp.einsum("sd,sf->df", mlp_in, pre_grad, preferred_element_type=jnp.float32)
        norm2_partial = jnp.einsum(
            "sf,df->sd", pre_grad, up_full, preferred_element_type=jnp.float32
        )
        normed2_share = column_share(normed2, share_start, share_width)
        norm2_share = lax.psum_scatter(norm2_partial, "tensor", scatter_dimension=1, tiled=True)
        hidden1_grad = grad_share + norm_back(norm2_share, normed2_share, inverse2, mlp_gain_share)
        branch_low = lax.all_gather(hidden1_grad.astype(jnp.bfloat16), "tensor", axis=1, tiled=True)
        output_grad = jnp.einsum(
            "sh,sd->hd", mixed_low, branch_low, preferred_element_type=jnp.float32
        )
        mixed_grad = split_heads(
            jnp.einsum(
                "sd,hd->sh", branch_low, output_full, preferred_element_type=jnp.float32
            ).astype(jnp.bfloat16)
        )
        scores_again = (
            jnp.einsum("hqd,hkd->hqk", query_heads, key_heads, preferred_element_type=jnp.float32)
            * score_scale
        )
        probs_again = jnp.exp(scores_again - log_total)
        probs_again_low = probs_again.astype(jnp.bfloat16)
        prob_grad = jnp.einsum(
            "hqd,hkd->hqk", mixed_grad, value_heads, preferred_element_type=jnp.float32
        )
        row_delta = jnp.sum(probs_again * prob_grad, axis=-1, keepdims=True)
        score_grad = (probs_again * (prob_grad - row_delta)).astype(jnp.bfloat16)
        query_grad = merge_heads(
            jnp.einsum("hqk,hkd->hqd", score_grad, key_heads, preferred_element_type=jnp.float32)
            * score_scale
        ).astype(jnp.bfloat16)
        key_grad = merge_heads(
            jnp.einsum("hqk,hqd->hkd", score_grad, query_heads, preferred_element_type=jnp.float32)
            * score_scale
        ).astype(jnp.bfloat16)
        value_grad = merge_heads(
            jnp.einsum(
                "hqk,hqd->hkd", probs_again_low, mixed_grad, preferred_element_type=jnp.float32
            )
        ).astype(jnp.bfloat16)
        query_w_grad = jnp.einsum(
            "sd,sh->dh", attn_in, query_grad, preferred_element_type=jnp.float32
        )
        key_w_grad = jnp.einsum("sd,sh->dh", attn_in, key_grad, preferred_element_type=jnp.float32)
        value_w_grad = jnp.einsum(
            "sd,sh->dh", attn_in, value_grad, preferred_element_type=jnp.float32
        )
        norm1_partial = jnp.einsum(
            "sh,dh->sd", query_grad, query_full, preferred_element_type=jnp.float32
        )
        norm1_partial = norm1_partial + jnp.einsum(
            "sh,dh->sd", key_grad, key_full, preferred_element_type=jnp.float32
        )
        norm1_partial = norm1_partial + jnp.einsum(
            "sh,dh->sd", value_grad, value_full, preferred_element_type=jnp.float32
        )
        norm1_share = lax.psum_scatter(
            norm1_partial.astype(jnp.bfloat16), "tensor", scatter_dimension=1, tiled=True
        ).astype(jnp.float32)
        normed1_share = column_share(normed1, share_start, share_width)
        grad_slots.append(
            (
                hidden1_grad + norm_back(norm1_share, normed1_share, inverse1, attn_gain_share)
            ).astype(jnp.bfloat16)
        )
        slot_grads = (
            query_w_grad,
            key_w_grad,
            value_w_grad,
            up_grad,
            output_grad,
            down_grad,
            jnp.sum(norm1_share * normed1_share, axis=0),
            jnp.sum(norm1_share, axis=0),
            jnp.sum(query_grad.astype(jnp.float32), axis=0),
            jnp.sum(value_grad.astype(jnp.float32), axis=0),
            jnp.sum(hidden1_grad, axis=0),
            jnp.sum(norm2_share * normed2_share, axis=0),
            jnp.sum(norm2_share, axis=0),
            jnp.sum(pre_grad.astype(jnp.float32), axis=0),
            jnp.sum(grad_share, axis=0),
        )
        grads_sum = (
            slot_grads if grads_sum is None else jax.tree.map(jnp.add, grads_sum, slot_grads)
        )
    row_grads = (
        lax.psum_scatter(grads_sum[0], "dp", scatter_dimension=0, tiled=True),
        lax.psum_scatter(grads_sum[1], "dp", scatter_dimension=0, tiled=True),
        lax.psum_scatter(grads_sum[2], "dp", scatter_dimension=0, tiled=True),
        lax.psum_scatter(grads_sum[3], "dp", scatter_dimension=0, tiled=True),
    )
    col_grads = (
        lax.psum_scatter(grads_sum[4], "dp", scatter_dimension=1, tiled=True),
        lax.psum_scatter(grads_sum[5], "dp", scatter_dimension=1, tiled=True),
    )
    small = lax.psum(
        (
            grads_sum[6],
            grads_sum[7],
            grads_sum[8],
            grads_sum[9],
            grads_sum[10],
            grads_sum[11],
            grads_sum[12],
            grads_sum[13],
            grads_sum[14],
        ),
        "dp",
    )
    return (
        jnp.stack(out_slots),
        jnp.stack(grad_slots),
        small[0],
        small[1],
        row_grads[0],
        small[2],
        row_grads[1],
        row_grads[2],
        small[3],
        col_grads[0],
        small[4],
        small[5],
        small[6],
        row_grads[3],
        small[7],
        col_grads[1],
        small[8],
    )


def solution(mesh):
    in_specs = (
        P("dp", None, "tensor"),
        P("dp"),
        P(),
        P(),
        P("dp", "tensor"),
        P("tensor"),
        P("dp", "tensor"),
        P("dp", "tensor"),
        P("tensor"),
        P("tensor", "dp"),
        P("tensor"),
        P(),
        P(),
        P("dp", "tensor"),
        P("tensor"),
        P("tensor", "dp"),
        P("tensor"),
        P("dp", None, "tensor"),
    )
    out_specs = (
        P("dp", None, "tensor"),
        P("dp", None, "tensor"),
        P("tensor"),
        P("tensor"),
        P("dp", "tensor"),
        P("tensor"),
        P("dp", "tensor"),
        P("dp", "tensor"),
        P("tensor"),
        P("tensor", "dp"),
        P("tensor"),
        P("tensor"),
        P("tensor"),
        P("dp", "tensor"),
        P("tensor"),
        P("tensor", "dp"),
        P("tensor"),
    )
    return jax.shard_map(local, mesh=mesh, in_specs=in_specs, out_specs=out_specs, check_vma=False)
```

profile of v0, /device:TPU:0, one launch (start us, length us, event | category | flops | bytes accessed | tf_op | source)
XLA Modules:
  0.0 1480.5 jit_solution(229131202090913659)
XLA Ops:
  11.3 34.3 %all_gather.67 = bf16[1152,288]{1,0:T(8,128)(2,1)S(1)} all-gather(bf16[144,288]{1,0:T(8,128)(2,1)S(1)} %copy-done.91), channel_id=1, replica_groups=mesh['dp'=8,'tensor'=4] {'dp'}, dimensions={0}, use_global_device_ids=true | all-gather | bytes 746496 | tf_op jit(solution)/shard_map/all_gather | solution.py:17
  45.6 32.7 %all_gather.68 = bf16[1152,288]{1,0:T(8,128)(2,1)S(1)} all-gather(bf16[144,288]{1,0:T(8,128)(2,1)S(1)} %copy-done.92), channel_id=1, replica_groups=mesh['dp'=8,'tensor'=4] {'dp'}, dimensions={0}, use_global_device_ids=true | all-gather | bytes 746496 | tf_op jit(solution)/shard_map/all_gather | solution.py:18
  78.3 32.3 %all_gather.69 = bf16[1152,288]{1,0:T(8,128)(2,1)S(1)} all-gather(bf16[144,288]{1,0:T(8,128)(2,1)S(1)} %copy-done.93), channel_id=1, replica_groups=mesh['dp'=8,'tensor'=4] {'dp'}, dimensions={0}, use_global_device_ids=true | all-gather | bytes 746496 | tf_op jit(solution)/shard_map/all_gather | solution.py:19
  110.6 32.1 %all_gather.70 = bf16[288,1152]{0,1:T(8,128)(2,1)S(1)} all-gather(bf16[288,144]{0,1:T(8,128)(2,1)} %param.27), channel_id=1, replica_groups=mesh['dp'=8,'tensor'=4] {'dp'}, dimensions={1}, use_global_device_ids=true | all-gather | bytes 746496 | tf_op jit(solution)/shard_map/all_gather | solution.py:23
  204.2 43.1 %reduce-scatter.27.cloned.1.call-done = f32[729,288]{0,1:T(8,128)} async-done(((f32[729,1152]{0,1:T(8,128)}), f32[729,288]{0,1:T(8,128)}) %reduce-scatter.27.cloned.1.call-update) | async-done | bytes 839824 | tf_op jit(solution)/shard_map/reduce_scatter | solution.py:127
  247.3 42.9 %reduce-scatter.19.cloned.1.call-done = f32[729,288]{0,1:T(8,128)} async-done(((f32[729,1152]{0,1:T(8,128)}), f32[729,288]{0,1:T(8,128)}) %reduce-scatter.19.cloned.1.call-update) | async-done | bytes 839824 | tf_op jit(solution)/shard_map/reduce_scatter | solution.py:127
  299.8 24.9 %all-gather.29.cloned.1.call-done = f32[729,1152]{0,1:T(8,128)} async-done(((f32[729,288]{0,1:T(8,128)}), f32[729,1152]{0,1:T(8,128)}) %all-gather.29.cloned.1.call-update) | async-done | bytes 3359248 | tf_op jit(solution)/shard_map/all_gather | solution.py:129
  330.3 51.8 %all-gather.23.cloned.1.call-done = bf16[1152,1076]{1,0:T(8,128)(2,1)} async-done(((bf16[144,1076]{1,0:T(8,128)(2,1)}), bf16[1152,1076]{1,0:T(8,128)(2,1)}) %all-gather.23.cloned.1.call-update) | async-done | bytes 2479120 | tf_op jit(solution)/shard_map/all_gather | solution.py:20
  387.6 16.2 %all-gather.47.cloned.1.call-done = bf16[1,729,1152]{1,2,0:T(8,128)(2,1)} async-done(((bf16[1,729,288]{1,2,0:T(8,128)(2,1)}), bf16[1,729,1152]{1,2,0:T(8,128)(2,1)}) %all-gather.47.cloned.1.call-update) | async-done | bytes 1679632 | tf_op jit(solution)/shard_map/all_gather | solution.py:92
  403.7 57.3 %all-gather.25.cloned.1.call-done = bf16[1076,1152]{0,1:T(8,128)(2,1)} async-done(((bf16[1076,144]{0,1:T(8,128)(2,1)}), bf16[1076,1152]{0,1:T(8,128)(2,1)}) %all-gather.25.cloned.1.call-update) | async-done | bytes 2479120 | tf_op jit(solution)/shard_map/all_gather | solution.py:24
  474.5 18.2 %all-gather.27.cloned.1.call-done = f32[729,1152]{0,1:T(8,128)} async-done(((f32[729,288]{0,1:T(8,128)}), f32[729,1152]{0,1:T(8,128)}) %all-gather.27.cloned.1.call-update) | async-done | bytes 3359248 | tf_op jit(solution)/shard_map/all_gather | solution.py:129
  503.4 11.6 all-gather.45.cloned.1.call-done
  528.4 19.5 %all-gather.21.cloned.1.call-done = f32[729,1152]{0,1:T(8,128)} async-done(((f32[729,288]{0,1:T(8,128)}), f32[729,1152]{0,1:T(8,128)}) %all-gather.21.cloned.1.call-update) | async-done | bytes 3359248 | tf_op jit(solution)/shard_map/all_gather | solution.py:129
  558.9 12.0 all-gather.43.cloned.1.call-done
  585.0 28.9 %reduce-scatter.39.cloned.1.call-done = f32[729,288]{0,1:T(8,128)} async-done(((f32[729,1152]{0,1:T(8,128)}), f32[729,288]{0,1:T(8,128)}) %reduce-scatter.39.cloned.1.call-update) | async-done | bytes 839824 | tf_op jit(solution)/shard_map/reduce_scatter | solution.py:150
  613.9 42.9 %reduce-scatter.35.cloned.1.call-done = f32[729,288]{0,1:T(8,128)} async-done(((f32[729,1152]{0,1:T(8,128)}), f32[729,288]{0,1:T(8,128)}) %reduce-scatter.35.cloned.1.call-update) | async-done | bytes 839824 | tf_op jit(solution)/shard_map/reduce_scatter | solution.py:150
  656.7 43.0 %reduce-scatter.31.cloned.1.call-done = f32[729,288]{0,1:T(8,128)} async-done(((f32[729,1152]{0,1:T(8,128)}), f32[729,288]{0,1:T(8,128)}) %reduce-scatter.31.cloned.1.call-update) | async-done | bytes 839824 | tf_op jit(solution)/shard_map/reduce_scatter | solution.py:150
  703.8 10.5 all-reduce.2
  755.4 10.2 multiply_convert_fusion.2
  782.8 7.7 multiply_reduce_fusion
  790.5 10.8 multiply_convert_fusion
  825.1 11.1 multiply_convert_fusion.1
  919.0 27.4 %reduce-scatter.41.cloned.1.call-done = bf16[729,288]{0,1:T(8,128)(2,1)} async-done(((bf16[729,1152]{0,1:T(8,128)(2,1)}), bf16[729,288]{0,1:T(8,128)(2,1)}) %reduce-scatter.41.cloned.1.call-update) | async-done | bytes 419920 | tf_op jit(solution)/shard_map/reduce_scatter | solution.py:201
  946.4 32.0 %reduce-scatter.37.cloned.1.call-done = bf16[729,288]{0,1:T(8,128)(2,1)} async-done(((bf16[729,1152]{0,1:T(8,128)(2,1)}), bf16[729,288]{0,1:T(8,128)(2,1)}) %reduce-scatter.37.cloned.1.call-update) | async-done | bytes 419920 | tf_op jit(solution)/shard_map/reduce_scatter | solution.py:201
  983.4 40.5 %all-reduce = (f32[288]{0:T(512)}, f32[288]{0:T(512)}, f32[288]{0:T(512)}, f32[288]{0:T(512)}, f32[288]{0:T(512)}, /*index=5*/f32[288]{0:T(512)}, f32[288]{0:T(512)}, f32[1076]{0:T(1024)}, f32[288]{0:T(512)}) all-reduce(f32[288]{0:T(512)} %add_add_fusion.8, f32[288]{0:T(512)} %add_add_fusion.7, ...), channel_id=1, replica_groups=mesh['dp'=8,'tensor'=4] {'dp'}, use_global_device_ids=true, to_apply=%region_60.0 | all-reduce | flops 3380 | bytes 27040 | tf_op jit(solution)/shard_map/psum | solution.py:240
  1023.9 12.2 all-reduce.1
  1045.0 42.1 %reduce-scatter.53.cloned.1.call-done = f32[1076,144]{0,1:T(8,128)} async-done(((f32[1076,1152]{0,1:T(8,128)}), f32[1076,144]{0,1:T(8,128)}) %reduce-scatter.53.cloned.1.call-update) | async-done | bytes 619792 | tf_op jit(solution)/shard_map/reduce_scatter | solution.py:238
  1087.2 108.6 %reduce-scatter.51.cloned.1.call-done = f32[144,1076]{1,0:T(8,128)} async-done(((f32[1152,1076]{1,0:T(8,128)}), f32[144,1076]{1,0:T(8,128)}) %reduce-scatter.51.cloned.1.call-update) | async-done | bytes 619792 | tf_op jit(solution)/shard_map/reduce_scatter | solution.py:234
  1195.7 69.7 %reduce-scatter.49.cloned.1.call-done = f32[288,144]{0,1:T(8,128)} async-done(((f32[288,1152]{0,1:T(8,128)}), f32[288,144]{0,1:T(8,128)}) %reduce-scatter.49.cloned.1.call-update) | async-done | bytes 165904 | tf_op jit(solution)/shard_map/reduce_scatter | solution.py:237
  1265.5 69.7 %reduce-scatter.47.cloned.1.call-done = f32[144,288]{1,0:T(8,128)} async-done(((f32[1152,288]{1,0:T(8,128)}), f32[144,288]{1,0:T(8,128)}) %reduce-scatter.47.cloned.1.call-update) | async-done | bytes 165904 | tf_op jit(solution)/shard_map/reduce_scatter | solution.py:233
  1335.2 69.2 %reduce-scatter.43.cloned.1.call-done = f32[144,288]{1,0:T(8,128)} async-done(((f32[1152,288]{1,0:T(8,128)}), f32[144,288]{1,0:T(8,128)}) %reduce-scatter.43.cloned.1.call-update) | async-done | bytes 165904 | tf_op jit(solution)/shard_map/reduce_scatter | solution.py:231
  1404.3 69.4 %reduce-scatter.45.cloned.1.call-done = f32[144,288]{1,0:T(8,128)} async-done(((f32[1152,288]{1,0:T(8,128)}), f32[144,288]{1,0:T(8,128)}) %reduce-scatter.45.cloned.1.call-update) | async-done | bytes 165904 | tf_op jit(solution)/shard_map/reduce_scatter | solution.py:232
  (542 shorter events, 328.8 us)
Async XLA Ops:
  7.2 135.5 %all-gather.39.cloned.1.call-start = ((), (), s32[]{:S(2)}) async-start(), calls=%async_computation.45 | async-start | bytes 2211840 | tf_op jit(solution)/shard_map/all_gather | solution.py:91
  9.7 152.9 %all-gather.41.cloned.1.call-start = ((), (), s32[]{:S(2)}) async-start(), calls=%async_computation.46 | async-start | bytes 2211840 | tf_op jit(solution)/shard_map/all_gather | solution.py:91
  10.5 172.1 %all-gather.37.cloned.1.call-start = ((), (), s32[]{:S(2)}) async-start(), calls=%async_computation.44 | async-start | bytes 2211840 | tf_op jit(solution)/shard_map/all_gather | solution.py:91
  11.2 193.0 %reduce-scatter.23.cloned.1.call-start = ((), (), s32[]{:S(2)}) async-start(), calls=%async_computation.23 | async-start | bytes 4423680 | tf_op jit(solution)/shard_map/reduce_scatter | solution.py:127
  162.1 85.2 %reduce-scatter.27.cloned.1.call-start = ((), (), s32[]{:S(2)}) async-start(), calls=%async_computation.26 | async-start | bytes 4423680 | tf_op jit(solution)/shard_map/reduce_scatter | solution.py:127
  182.4 107.8 %reduce-scatter.19.cloned.1.call-start = ((), (), s32[]{:S(2)}) async-start(), calls=%async_computation.18 | async-start | bytes 4423680 | tf_op jit(solution)/shard_map/reduce_scatter | solution.py:127
  202.4 122.3 %all-gather.29.cloned.1.call-start = ((), (), s32[]{:S(2)}) async-start(), calls=%async_computation.27 | async-start | bytes 4423680 | tf_op jit(solution)/shard_map/all_gather | solution.py:129
  293.8 88.4 %all-gather.23.cloned.1.call-start = ((), (), s32[]{:S(2)}) async-start(), calls=%async_computation.20 | async-start | bytes 2985984 | tf_op jit(solution)/shard_map/all_gather | solution.py:20
  294.5 109.2 %all-gather.47.cloned.1.call-start = ((), (), s32[]{:S(2)}) async-start(), calls=%async_computation.49 | async-start | bytes 2211840 | tf_op jit(solution)/shard_map/all_gather | solution.py:92
  295.7 165.4 %all-gather.25.cloned.1.call-start = ((), (), s32[]{:S(2)}) async-start(), calls=%async_computation.21 | async-start | bytes 2985984 | tf_op jit(solution)/shard_map/all_gather | solution.py:24
  296.3 196.4 %all-gather.27.cloned.1.call-start = ((), (), s32[]{:S(2)}) async-start(), calls=%async_computation.24 | async-start | bytes 4423680 | tf_op jit(solution)/shard_map/all_gather | solution.py:129
  297.0 217.9 %all-gather.45.cloned.1.call-start = ((), (), s32[]{:S(2)}) async-start(), calls=%async_computation.48 | async-start | bytes 2211840 | tf_op jit(solution)/shard_map/all_gather | solution.py:92
  297.6 250.4 %all-gather.21.cloned.1.call-start = ((), (), s32[]{:S(2)}) async-start(), calls=%async_computation.19 | async-start | bytes 4423680 | tf_op jit(solution)/shard_map/all_gather | solution.py:129
  298.3 272.5 %all-gather.43.cloned.1.call-start = ((), (), s32[]{:S(2)}) async-start(), calls=%async_computation.47 | async-start | bytes 2211840 | tf_op jit(solution)/shard_map/all_gather | solution.py:92
  298.9 314.9 %reduce-scatter.39.cloned.1.call-start = ((), (), s32[]{:S(2)}) async-start(), calls=%async_computation.35 | async-start | bytes 4423680 | tf_op jit(solution)/shard_map/reduce_scatter | solution.py:150
  474.0 182.7 %reduce-scatter.35.cloned.1.call-start = ((), (), s32[]{:S(2)}) async-start(), calls=%async_computation.32 | async-start | bytes 4423680 | tf_op jit(solution)/shard_map/reduce_scatter | solution.py:150
  528.2 171.6 %reduce-scatter.31.cloned.1.call-start = ((), (), s32[]{:S(2)}) async-start(), calls=%async_computation.29 | async-start | bytes 4423680 | tf_op jit(solution)/shard_map/reduce_scatter | solution.py:150
  584.0 161.5 %all-gather.31.cloned.1.call-start = ((), (), s32[]{:S(2)}) async-start(), calls=%async_computation.30 | async-start | bytes 2211840 | tf_op jit(solution)/shard_map/all_gather | solution.py:152
  719.1 61.3 %all-gather.35.cloned.1.call-start = ((), (), s32[]{:S(2)}) async-start(), calls=%async_computation.36 | async-start | bytes 2211840 | tf_op jit(solution)/shard_map/all_gather | solution.py:152
  720.0 95.8 %all-gather.33.cloned.1.call-start = ((), (), s32[]{:S(2)}) async-start(), calls=%async_computation.33 | async-start | bytes 2211840 | tf_op jit(solution)/shard_map/all_gather | solution.py:152
  724.0 179.7 %reduce-scatter.21.cloned.1.call-start = ((), (), s32[]{:S(2)}) async-start(), calls=%async_computation.22 | async-start | bytes 2211840 | tf_op jit(solution)/shard_map/reduce_scatter | solution.py:136
  730.8 172.8 %reduce-scatter.25.cloned.1.call-start = ((), (), s32[]{:S(2)}) async-start(), calls=%async_computation.25 | async-start | bytes 2211840 | tf_op jit(solution)/shard_map/reduce_scatter | solution.py:136
  737.5 166.2 %reduce-scatter.29.cloned.1.call-start = ((), (), s32[]{:S(2)}) async-start(), calls=%async_computation.28 | async-start | bytes 2211840 | tf_op jit(solution)/shard_map/reduce_scatter | solution.py:136
  745.1 173.9 %reduce-scatter.33.cloned.1.call-start = ((), (), s32[]{:S(2)}) async-start(), calls=%async_computation.31 | async-start | bytes 2211840 | tf_op jit(solution)/shard_map/reduce_scatter | solution.py:201
  780.1 166.3 %reduce-scatter.41.cloned.1.call-start = ((), (), s32[]{:S(2)}) async-start(), calls=%async_computation.37 | async-start | bytes 2211840 | tf_op jit(solution)/shard_map/reduce_scatter | solution.py:201
  815.4 163.0 %reduce-scatter.37.cloned.1.call-start = ((), (), s32[]{:S(2)}) async-start(), calls=%async_computation.34 | async-start | bytes 2211840 | tf_op jit(solution)/shard_map/reduce_scatter | solution.py:201
  850.3 236.9 %reduce-scatter.53.cloned.1.call-start = ((), (), s32[]{:S(2)}) async-start(), calls=%async_computation.43 | async-start | bytes 5971968 | tf_op jit(solution)/shard_map/reduce_scatter | solution.py:238
  863.6 332.2 %reduce-scatter.51.cloned.1.call-start = ((), (), s32[]{:S(2)}) async-start(), calls=%async_computation.42 | async-start | bytes 5971968 | tf_op jit(solution)/shard_map/reduce_scatter | solution.py:234
  877.9 387.6 %reduce-scatter.49.cloned.1.call-start = ((), (), s32[]{:S(2)}) async-start(), calls=%async_computation.41 | async-start | bytes 1990656 | tf_op jit(solution)/shard_map/reduce_scatter | solution.py:237
  885.5 449.7 %reduce-scatter.47.cloned.1.call-start = ((), (), s32[]{:S(2)}) async-start(), calls=%async_computation.40 | async-start | bytes 1990656 | tf_op jit(solution)/shard_map/reduce_scatter | solution.py:233
  892.8 511.6 %reduce-scatter.43.cloned.1.call-start = ((), (), s32[]{:S(2)}) async-start(), calls=%async_computation.38 | async-start | bytes 1990656 | tf_op jit(solution)/shard_map/reduce_scatter | solution.py:231
  902.3 571.5 %reduce-scatter.45.cloned.1.call-start = ((), (), s32[]{:S(2)}) async-start(), calls=%async_computation.39 | async-start | bytes 1990656 | tf_op jit(solution)/shard_map/reduce_scatter | solution.py:232
  (160 other events, 2436.1 us)
Sparse Core Ops, SparseCore 0:
  10.2 23.4 all-gather.38
  35.8 20.7 all-gather.40
  58.7 20.7 all-gather.36
  162.2 41.9 reduce-scatter.22
  206.8 40.4 reduce-scatter.26
  249.7 40.4 reduce-scatter.18
  293.9 30.7 all-gather.28
  327.1 55.0 all-gather.22
  384.4 19.3 all-gather.46
  406.0 55.0 all-gather.24
  463.3 29.3 all-gather.26
  494.1 20.7 all-gather.44
  517.1 30.7 all-gather.20
  550.0 20.7 all-gather.42
  573.4 40.4 reduce-scatter.38
  616.3 40.4 reduce-scatter.34
  659.3 40.4 reduce-scatter.30
  719.2 21.8 all-gather.30
  743.2 20.7 all-gather.34
  765.4 20.7 all-gather.32
  788.8 29.4 reduce-scatter.20
  821.1 29.3 reduce-scatter.24
  853.0 29.3 reduce-scatter.28
  885.0 29.3 reduce-scatter.32
  917.0 29.3 reduce-scatter.40
  949.0 29.3 reduce-scatter.36
  982.5 104.6 reduce-scatter.52
  1091.8 103.9 reduce-scatter.50
  1199.8 65.6 reduce-scatter.48
  1269.8 65.3 reduce-scatter.46
  1339.2 65.0 reduce-scatter.42
  1408.8 64.9 reduce-scatter.44
where the time goes:
time: 1490 us; the launch traced here: 1480 us
  waiting for transfers between devices  908 us (61%)
  matrix products  214 us (14%)
  blocking collectives  195 us (13%)
  other arithmetic  108 us (7%)
  local copies, waits for them, and re-layouts  34.3 us (2%)
  between operations  17 us (1%)
    reduce_scatter x3, waiting for transfers between devices, local(): lax.psum_scatter(norm2_partial, 'tensor', scatter_dimension=1, tiled=True)  115 us
    reduce_scatter x1, waiting for transfers between devices, local(): lax.psum_scatter(grads_sum[3], 'dp', scatter_dimension=0, tiled=True)  109 us
    reduce_scatter x3, waiting for transfers between devices, local(): lax.psum_scatter(attn_partial, 'tensor', scatter_dimension=1, tiled=True)  87.7 us
    reduce_scatter x1, waiting for transfers between devices, local(): lax.psum_scatter(grads_sum[4], 'dp', scatter_dimension=1, tiled=True)  69.7 us
    reduce_scatter x1, waiting for transfers between devices, local(): lax.psum_scatter(grads_sum[2], 'dp', scatter_dimension=0, tiled=True)  69.7 us
    reduce_scatter x1, waiting for transfers between devices, local(): lax.psum_scatter(grads_sum[1], 'dp', scatter_dimension=0, tiled=True)  69.4 us
    reduce_scatter x1, waiting for transfers between devices, local(): lax.psum_scatter(grads_sum[0], 'dp', scatter_dimension=0, tiled=True)  69.2 us
    all_gather x3, waiting for transfers between devices, local(): hidden1_full = lax.all_gather(hidden1_share, 'tensor', axis=1, tiled=True)  62.6 us
  transfers between devices with their start and end apart: 32, of which 22 were waited for; matrix products, arithmetic and copies ran while one was open for 21% of the time, Pallas kernels for 0%

commit v1 on v0

--- a/solution.py
+++ b/solution.py
@@ -8,6 +8,19 @@
 EPSILON = 1e-06
 
 
+def collect(x, axis, dim):
+    ways = lax.axis_size(axis)
+    up = [(d, (d + 1) % ways) for d in range(ways)]
+    down = [(d, (d - 1) % ways) for d in range(ways)]
+    earlier, later = ([x], [x])
+    for _ in range(ways // 2):
+        earlier.append(lax.ppermute(earlier[-1], axis, up))
+    for _ in range((ways - 1) // 2):
+        later.append(lax.ppermute(later[-1], axis, down))
+    line = jnp.concatenate([*earlier[::-1], *later[1:]], axis=dim)
+    return jnp.roll(line, (lax.axis_index(axis) - ways // 2) * x.shape[dim], axis=dim)
+
+
 def gelu_tanh(value):
     return jax.nn.gelu(value, approximate=True)
 
@@ -17,7 +30,7 @@
         lax.all_gather(query_weight, "dp", axis=0, tiled=True),
         lax.all_gather(key_weight, "dp", axis=0, tiled=True),
         lax.all_gather(value_weight, "dp", axis=0, tiled=True),
-        lax.all_gather(up_weight, "dp", axis=0, tiled=True),
+        collect(up_weight, "dp", 0),
     )
     col_parts = (
         lax.all_gather(output_weight, "dp", axis=1, tiled=True),

time: 1490 us -> 1430 us (0.960)
  waiting for transfers between devices: 908 us -> 820 us
  starting transfers between devices: 4.31 us -> 32.5 us
    all_gather x1 -> x0, waiting for transfers between devices: 51.8 us -> none  [fetch_weights(): lax.all_gather(up_weight, 'dp', axis=0, tiled=True)]
    ppermute x0 -> x7, waiting for transfers between devices: none -> 30.4 us  [the longest x4 27 us: collect(): earlier.append(lax.ppermute(earlier[-1], axis, up))]
    ppermute x0 -> x7, starting transfers between devices: none -> 28.9 us  [the longest x3 22.4 us: collect(): later.append(lax.ppermute(later[-1], axis, down))]
    all_gather x3, waiting for transfers between devices: 62.6 us -> 37.4 us  [local(): hidden1_full = lax.all_gather(hidden1_share, 'tensor', axis=1, tiled=True)]
    all_gather x1, waiting for transfers between devices: 57.3 us -> 32.6 us  [fetch_weights(): lax.all_gather(down_weight, 'dp', axis=1, tiled=True)]
    all_gather x3, waiting for transfers between devices: 39.7 us -> 24 us  [local(): lax.all_gather(cotangent[slot_index], 'tensor', axis=1, tiled=True)]
    unnamed x320 -> x337, local copies, waits for them, and re-layouts: 27.7 us -> 30.2 us
  transfers between devices with their start and end apart: 32 -> 38, of which waited for: 22 -> 24; matrix products, arithmetic and copies ran while one was open for 21% -> 22% of each run, Pallas kernels for 0% -> 0%
where the time goes in v1:
time: 1430 us; the launch traced here: 1420 us
  waiting for transfers between devices  820 us (57%)
  matrix products  212 us (15%)
  blocking collectives  195 us (14%)
  other arithmetic  112 us (8%)
  local copies, waits for them, and re-layouts  36.8 us (3%)
  starting transfers between devices  32.5 us (2%)
  between operations  17.4 us (1%)
    reduce_scatter x3, waiting for transfers between devices, local(): lax.psum_scatter(norm2_partial, 'tensor', scatter_dimension=1, tiled=True)  115 us
    reduce_scatter x1, waiting for transfers between devices, local(): lax.psum_scatter(grads_sum[3], 'dp', scatter_dimension=0, tiled=True)  108 us
    reduce_scatter x3, waiting for transfers between devices, local(): lax.psum_scatter(attn_partial, 'tensor', scatter_dimension=1, tiled=True)  88 us
    reduce_scatter x1, waiting for transfers between devices, local(): lax.psum_scatter(grads_sum[4], 'dp', scatter_dimension=1, tiled=True)  70.2 us
    reduce_scatter x1, waiting for transfers between devices, local(): lax.psum_scatter(grads_sum[2], 'dp', scatter_dimension=0, tiled=True)  69.6 us
    reduce_scatter x1, waiting for transfers between devices, local(): lax.psum_scatter(grads_sum[1], 'dp', scatter_dimension=0, tiled=True)  69.3 us
    reduce_scatter x1, waiting for transfers between devices, local(): lax.psum_scatter(grads_sum[0], 'dp', scatter_dimension=0, tiled=True)  69.1 us
    reduce_scatter x3, waiting for transfers between devices, local(): lax.psum_scatter(norm1_partial.astype(jnp.bfloat16), 'tensor', scatter_di...  59.7 us
  transfers between devices with their start and end apart: 38, of which 24 were waited for; matrix products, arithmetic and copies ran while one was open for 22% of the time, Pallas kernels for 0%

profile of v1, /device:TPU:0, one launch (start us, length us, event | category | flops | bytes accessed | tf_op | source)
XLA Modules:
  0.0 1424.7 jit_solution(10284635923003014807)
XLA Ops:
  11.3 34.3 %all_gather.62 = bf16[1152,288]{1,0:T(8,128)(2,1)S(1)} all-gather(bf16[144,288]{1,0:T(8,128)(2,1)S(1)} %copy-done.99), channel_id=1, replica_groups=mesh['dp'=8,'tensor'=4] {'dp'}, dimensions={0}, use_global_device_ids=true | all-gather | bytes 746496 | tf_op jit(solution)/shard_map/all_gather | solution.py:30
  45.6 32.7 %all_gather.63 = bf16[1152,288]{1,0:T(8,128)(2,1)S(1)} all-gather(bf16[144,288]{1,0:T(8,128)(2,1)S(1)} %copy-done.100), channel_id=1, replica_groups=mesh['dp'=8,'tensor'=4] {'dp'}, dimensions={0}, use_global_device_ids=true | all-gather | bytes 746496 | tf_op jit(solution)/shard_map/all_gather | solution.py:31
  78.3 32.3 %all_gather.64 = bf16[1152,288]{1,0:T(8,128)(2,1)S(1)} all-gather(bf16[144,288]{1,0:T(8,128)(2,1)S(1)} %copy-done.101), channel_id=1, replica_groups=mesh['dp'=8,'tensor'=4] {'dp'}, dimensions={0}, use_global_device_ids=true | all-gather | bytes 746496 | tf_op jit(solution)/shard_map/all_gather | solution.py:32
  110.6 32.1 %all_gather.65 = bf16[288,1152]{0,1:T(8,128)(2,1)S(1)} all-gather(bf16[288,144]{0,1:T(8,128)(2,1)} %param.29), channel_id=1, replica_groups=mesh['dp'=8,'tensor'=4] {'dp'}, dimensions={1}, use_global_device_ids=true | all-gather | bytes 746496 | tf_op jit(solution)/shard_map/all_gather | solution.py:36
  204.2 43.1 %reduce-scatter.27.cloned.1.call-done = f32[729,288]{0,1:T(8,128)} async-done(((f32[729,1152]{0,1:T(8,128)}), f32[729,288]{0,1:T(8,128)}) %reduce-scatter.27.cloned.1.call-update) | async-done | bytes 839824 | tf_op jit(solution)/shard_map/reduce_scatter | solution.py:140
  247.2 42.9 %reduce-scatter.19.cloned.1.call-done = f32[729,288]{0,1:T(8,128)} async-done(((f32[729,1152]{0,1:T(8,128)}), f32[729,288]{0,1:T(8,128)}) %reduce-scatter.19.cloned.1.call-update) | async-done | bytes 839824 | tf_op jit(solution)/shard_map/reduce_scatter | solution.py:140
  299.1 10.8 collective-permute-done
  314.6 8.9 collective-permute-done.1
  325.9 8.3 collective-permute-start.5
  342.1 9.4 collective-permute-start.6
  372.5 32.6 %all-gather.22.cloned.1.call-done = bf16[1076,1152]{0,1:T(8,128)(2,1)} async-done(((bf16[1076,144]{0,1:T(8,128)(2,1)}), bf16[1076,1152]{0,1:T(8,128)(2,1)}) %all-gather.22.cloned.1.call-update) | async-done | bytes 2479120 | tf_op jit(solution)/shard_map/all_gather | solution.py:37
  418.4 18.2 %all-gather.24.cloned.1.call-done = f32[729,1152]{0,1:T(8,128)} async-done(((f32[729,288]{0,1:T(8,128)}), f32[729,1152]{0,1:T(8,128)}) %all-gather.24.cloned.1.call-update) | async-done | bytes 3359248 | tf_op jit(solution)/shard_map/all_gather | solution.py:142
  447.3 11.7 all-gather.42.cloned.1.call-done
  472.7 19.2 %all-gather.20.cloned.1.call-done = f32[729,1152]{0,1:T(8,128)} async-done(((f32[729,288]{0,1:T(8,128)}), f32[729,1152]{0,1:T(8,128)}) %all-gather.20.cloned.1.call-update) | async-done | bytes 3359248 | tf_op jit(solution)/shard_map/all_gather | solution.py:142
  502.6 12.3 all-gather.40.cloned.1.call-done
  529.1 28.9 %reduce-scatter.39.cloned.1.call-done = f32[729,288]{0,1:T(8,128)} async-done(((f32[729,1152]{0,1:T(8,128)}), f32[729,288]{0,1:T(8,128)}) %reduce-scatter.39.cloned.1.call-update) | async-done | bytes 839824 | tf_op jit(solution)/shard_map/reduce_scatter | solution.py:163
  558.0 42.9 %reduce-scatter.35.cloned.1.call-done = f32[729,288]{0,1:T(8,128)} async-done(((f32[729,1152]{0,1:T(8,128)}), f32[729,288]{0,1:T(8,128)}) %reduce-scatter.35.cloned.1.call-update) | async-done | bytes 839824 | tf_op jit(solution)/shard_map/reduce_scatter | solution.py:163
  600.8 43.0 %reduce-scatter.31.cloned.1.call-done = f32[729,288]{0,1:T(8,128)} async-done(((f32[729,1152]{0,1:T(8,128)}), f32[729,288]{0,1:T(8,128)}) %reduce-scatter.31.cloned.1.call-update) | async-done | bytes 839824 | tf_op jit(solution)/shard_map/reduce_scatter | solution.py:163
  647.9 10.5 all-reduce.2
  699.3 10.2 multiply_convert_fusion.2
  734.6 10.9 multiply_convert_fusion
  769.2 11.0 multiply_convert_fusion.1
  862.9 27.5 %reduce-scatter.41.cloned.1.call-done = bf16[729,288]{0,1:T(8,128)(2,1)} async-done(((bf16[729,1152]{0,1:T(8,128)(2,1)}), bf16[729,288]{0,1:T(8,128)(2,1)}) %reduce-scatter.41.cloned.1.call-update) | async-done | bytes 419920 | tf_op jit(solution)/shard_map/reduce_scatter | solution.py:214
  890.4 32.2 %reduce-scatter.37.cloned.1.call-done = bf16[729,288]{0,1:T(8,128)(2,1)} async-done(((bf16[729,1152]{0,1:T(8,128)(2,1)}), bf16[729,288]{0,1:T(8,128)(2,1)}) %reduce-scatter.37.cloned.1.call-update) | async-done | bytes 419920 | tf_op jit(solution)/shard_map/reduce_scatter | solution.py:214
  927.5 40.5 %all-reduce = (f32[288]{0:T(512)}, f32[288]{0:T(512)}, f32[288]{0:T(512)}, f32[288]{0:T(512)}, f32[288]{0:T(512)}, /*index=5*/f32[288]{0:T(512)}, f32[288]{0:T(512)}, f32[1076]{0:T(1024)}, f32[288]{0:T(512)}) all-reduce(f32[288]{0:T(512)} %add_add_fusion.8, f32[288]{0:T(512)} %add_add_fusion.7, ...), channel_id=1, replica_groups=mesh['dp'=8,'tensor'=4] {'dp'}, use_global_device_ids=true, to_apply=%region_60.62 | all-reduce | flops 3380 | bytes 27040 | tf_op jit(solution)/shard_map/psum | solution.py:253
  968.0 12.2 all-reduce.1
  989.1 42.0 %reduce-scatter.53.cloned.1.call-done = f32[1076,144]{0,1:T(8,128)} async-done(((f32[1076,1152]{0,1:T(8,128)}), f32[1076,144]{0,1:T(8,128)}) %reduce-scatter.53.cloned.1.call-update) | async-done | bytes 619792 | tf_op jit(solution)/shard_map/reduce_scatter | solution.py:251
  1031.1 108.4 %reduce-scatter.51.cloned.1.call-done = f32[144,1076]{1,0:T(8,128)} async-done(((f32[1152,1076]{1,0:T(8,128)}), f32[144,1076]{1,0:T(8,128)}) %reduce-scatter.51.cloned.1.call-update) | async-done | bytes 619792 | tf_op jit(solution)/shard_map/reduce_scatter | solution.py:247
  1139.5 70.2 %reduce-scatter.49.cloned.1.call-done = f32[288,144]{0,1:T(8,128)} async-done(((f32[288,1152]{0,1:T(8,128)}), f32[288,144]{0,1:T(8,128)}) %reduce-scatter.49.cloned.1.call-update) | async-done | bytes 165904 | tf_op jit(solution)/shard_map/reduce_scatter | solution.py:250
  1209.7 69.6 %reduce-scatter.47.cloned.1.call-done = f32[144,288]{1,0:T(8,128)} async-done(((f32[1152,288]{1,0:T(8,128)}), f32[144,288]{1,0:T(8,128)}) %reduce-scatter.47.cloned.1.call-update) | async-done | bytes 165904 | tf_op jit(solution)/shard_map/reduce_scatter | solution.py:246
  1279.3 69.1 %reduce-scatter.43.cloned.1.call-done = f32[144,288]{1,0:T(8,128)} async-done(((f32[1152,288]{1,0:T(8,128)}), f32[144,288]{1,0:T(8,128)}) %reduce-scatter.43.cloned.1.call-update) | async-done | bytes 165904 | tf_op jit(solution)/shard_map/reduce_scatter | solution.py:244
  1348.4 69.3 %reduce-scatter.45.cloned.1.call-done = f32[144,288]{1,0:T(8,128)} async-done(((f32[1152,288]{1,0:T(8,128)}), f32[144,288]{1,0:T(8,128)}) %reduce-scatter.45.cloned.1.call-update) | async-done | bytes 165904 | tf_op jit(solution)/shard_map/reduce_scatter | solution.py:245
  (572 shorter events, 360.2 us)
Async XLA Ops:
  7.2 135.5 %all-gather.36.cloned.1.call-start = ((), (), s32[]{:S(2)}) async-start(), calls=%async_computation.44 | async-start | bytes 2211840 | tf_op jit(solution)/shard_map/all_gather | solution.py:104
  9.7 152.6 %all-gather.38.cloned.1.call-start = ((), (), s32[]{:S(2)}) async-start(), calls=%async_computation.45 | async-start | bytes 2211840 | tf_op jit(solution)/shard_map/all_gather | solution.py:104
  10.5 171.8 %all-gather.34.cloned.1.call-start = ((), (), s32[]{:S(2)}) async-start(), calls=%async_computation.43 | async-start | bytes 2211840 | tf_op jit(solution)/shard_map/all_gather | solution.py:104
  11.2 193.0 %reduce-scatter.23.cloned.1.call-start = ((), (), s32[]{:S(2)}) async-start(), calls=%async_computation.22 | async-start | bytes 4423680 | tf_op jit(solution)/shard_map/reduce_scatter | solution.py:140
  162.0 85.2 %reduce-scatter.27.cloned.1.call-start = ((), (), s32[]{:S(2)}) async-start(), calls=%async_computation.25 | async-start | bytes 4423680 | tf_op jit(solution)/shard_map/reduce_scatter | solution.py:140
  182.0 108.1 %reduce-scatter.19.cloned.1.call-start = ((), (), s32[]{:S(2)}) async-start(), calls=%async_computation.18 | async-start | bytes 4423680 | tf_op jit(solution)/shard_map/reduce_scatter | solution.py:140
  202.1 161.3 %all-gather.26.cloned.1.call-start = ((), (), s32[]{:S(2)}) async-start(), calls=%async_computation.26 | async-start | bytes 4423680 | tf_op jit(solution)/shard_map/all_gather | solution.py:142
  293.7 78.7 %all-gather.44.cloned.1.call-start = ((), (), s32[]{:S(2)}) async-start(), calls=%async_computation.48 | async-start | bytes 2211840 | tf_op jit(solution)/shard_map/all_gather | solution.py:105
  294.9 110.2 %all-gather.22.cloned.1.call-start = ((), (), s32[]{:S(2)}) async-start(), calls=%async_computation.20 | async-start | bytes 2985984 | tf_op jit(solution)/shard_map/all_gather | solution.py:37
  295.6 140.9 %all-gather.24.cloned.1.call-start = ((), (), s32[]{:S(2)}) async-start(), calls=%async_computation.23 | async-start | bytes 4423680 | tf_op jit(solution)/shard_map/all_gather | solution.py:142
  296.2 162.8 %all-gather.42.cloned.1.call-start = ((), (), s32[]{:S(2)}) async-start(), calls=%async_computation.47 | async-start | bytes 2211840 | tf_op jit(solution)/shard_map/all_gather | solution.py:105
  297.0 194.9 %all-gather.20.cloned.1.call-start = ((), (), s32[]{:S(2)}) async-start(), calls=%async_computation.19 | async-start | bytes 4423680 | tf_op jit(solution)/shard_map/all_gather | solution.py:142
  297.5 217.4 %all-gather.40.cloned.1.call-start = ((), (), s32[]{:S(2)}) async-start(), calls=%async_computation.46 | async-start | bytes 2211840 | tf_op jit(solution)/shard_map/all_gather | solution.py:105
  325.9 16.1 %collective-permute-start.5 = (bf16[144,1076]{1,0:T(8,128)(2,1)S(1)}, bf16[144,1076]{1,0:T(8,128)(2,1)S(1)}, u32[]{:S(2)}, u32[]{:S(2)}) collective-permute-start(bf16[144,1076]{1,0:T(8,128)(2,1)S(1)} %collective-permute-done.4), channel_id=1, source_target_pairs={{0,28},{4,0},{8,4},{12,8},{16,12},{20,16},{24,20},{28,24},{1,29},{... | collective-permute-start | bytes 929672 | tf_op jit(solution)/shard_map/ppermute | solution.py:19
  341.3 216.6 %reduce-scatter.39.cloned.1.call-start = ((), (), s32[]{:S(2)}) async-start(), calls=%async_computation.34 | async-start | bytes 4423680 | tf_op jit(solution)/shard_map/reduce_scatter | solution.py:163
  418.3 182.5 %reduce-scatter.35.cloned.1.call-start = ((), (), s32[]{:S(2)}) async-start(), calls=%async_computation.31 | async-start | bytes 4423680 | tf_op jit(solution)/shard_map/reduce_scatter | solution.py:163
  472.2 171.6 %reduce-scatter.31.cloned.1.call-start = ((), (), s32[]{:S(2)}) async-start(), calls=%async_computation.28 | async-start | bytes 4423680 | tf_op jit(solution)/shard_map/reduce_scatter | solution.py:163
  528.1 161.3 %all-gather.28.cloned.1.call-start = ((), (), s32[]{:S(2)}) async-start(), calls=%async_computation.29 | async-start | bytes 2211840 | tf_op jit(solution)/shard_map/all_gather | solution.py:165
  663.2 61.2 %all-gather.32.cloned.1.call-start = ((), (), s32[]{:S(2)}) async-start(), calls=%async_computation.35 | async-start | bytes 2211840 | tf_op jit(solution)/shard_map/all_gather | solution.py:165
  664.1 95.7 %all-gather.30.cloned.1.call-start = ((), (), s32[]{:S(2)}) async-start(), calls=%async_computation.32 | async-start | bytes 2211840 | tf_op jit(solution)/shard_map/all_gather | solution.py:165
  668.1 179.4 %reduce-scatter.21.cloned.1.call-start = ((), (), s32[]{:S(2)}) async-start(), calls=%async_computation.21 | async-start | bytes 2211840 | tf_op jit(solution)/shard_map/reduce_scatter | solution.py:149
  674.9 172.6 %reduce-scatter.25.cloned.1.call-start = ((), (), s32[]{:S(2)}) async-start(), calls=%async_computation.24 | async-start | bytes 2211840 | tf_op jit(solution)/shard_map/reduce_scatter | solution.py:149
  681.6 165.9 %reduce-scatter.29.cloned.1.call-start = ((), (), s32[]{:S(2)}) async-start(), calls=%async_computation.27 | async-start | bytes 2211840 | tf_op jit(solution)/shard_map/reduce_scatter | solution.py:149
  689.1 173.7 %reduce-scatter.33.cloned.1.call-start = ((), (), s32[]{:S(2)}) async-start(), calls=%async_computation.30 | async-start | bytes 2211840 | tf_op jit(solution)/shard_map/reduce_scatter | solution.py:214
  724.0 166.4 %reduce-scatter.41.cloned.1.call-start = ((), (), s32[]{:S(2)}) async-start(), calls=%async_computation.36 | async-start | bytes 2211840 | tf_op jit(solution)/shard_map/reduce_scatter | solution.py:214
  759.6 163.0 %reduce-scatter.37.cloned.1.call-start = ((), (), s32[]{:S(2)}) async-start(), calls=%async_computation.33 | async-start | bytes 2211840 | tf_op jit(solution)/shard_map/reduce_scatter | solution.py:214
  794.4 236.7 %reduce-scatter.53.cloned.1.call-start = ((), (), s32[]{:S(2)}) async-start(), calls=%async_computation.42 | async-start | bytes 5971968 | tf_op jit(solution)/shard_map/reduce_scatter | solution.py:251
  807.5 332.0 %reduce-scatter.51.cloned.1.call-start = ((), (), s32[]{:S(2)}) async-start(), calls=%async_computation.41 | async-start | bytes 5971968 | tf_op jit(solution)/shard_map/reduce_scatter | solution.py:247
  821.8 387.9 %reduce-scatter.49.cloned.1.call-start = ((), (), s32[]{:S(2)}) async-start(), calls=%async_computation.40 | async-start | bytes 1990656 | tf_op jit(solution)/shard_map/reduce_scatter | solution.py:250
  829.4 449.9 %reduce-scatter.47.cloned.1.call-start = ((), (), s32[]{:S(2)}) async-start(), calls=%async_computation.39 | async-start | bytes 1990656 | tf_op jit(solution)/shard_map/reduce_scatter | solution.py:246
  836.6 511.8 %reduce-scatter.43.cloned.1.call-start = ((), (), s32[]{:S(2)}) async-start(), calls=%async_computation.37 | async-start | bytes 1990656 | tf_op jit(solution)/shard_map/reduce_scatter | solution.py:244
  846.1 571.6 %reduce-scatter.45.cloned.1.call-start = ((), (), s32[]{:S(2)}) async-start(), calls=%async_computation.38 | async-start | bytes 1990656 | tf_op jit(solution)/shard_map/reduce_scatter | solution.py:245
  (171 other events, 2446.5 us)
Sparse Core Ops, SparseCore 0:
  10.2 23.4 all-gather.35
  35.8 20.7 all-gather.37
  58.7 20.7 all-gather.33
  162.2 41.9 reduce-scatter.22
  206.8 40.4 reduce-scatter.26
  249.7 40.4 reduce-scatter.18
  293.9 30.7 all-gather.25
  326.9 20.7 all-gather.43
  350.1 55.0 all-gather.21
  407.2 29.3 all-gather.23
  438.2 20.7 all-gather.41
  461.1 30.7 all-gather.19
  494.1 20.7 all-gather.39
  517.5 40.4 reduce-scatter.38
  560.4 40.4 reduce-scatter.34
  603.4 40.4 reduce-scatter.30
  663.3 21.8 all-gather.27
  687.2 20.7 all-gather.31
  709.6 20.7 all-gather.29
  732.8 29.3 reduce-scatter.20
  765.0 29.3 reduce-scatter.24
  797.0 29.3 reduce-scatter.28
  829.1 29.3 reduce-scatter.32
  861.0 29.3 reduce-scatter.40
  893.1 29.3 reduce-scatter.36
  926.6 104.5 reduce-scatter.52
  1035.6 103.9 reduce-scatter.50
  1143.6 66.1 reduce-scatter.48
  1214.1 65.1 reduce-scatter.46
  1283.2 65.1 reduce-scatter.42
  1352.8 64.7 reduce-scatter.44
